TPU v7x, 256 devices: a whole 4x4x8 slice. The times are simulated.
256 devices in a mesh: dp: 2 (over core), ctx: 8 (over z), tp: 16 (over y, x).
Axes of the slice: x: 4, y: 4, z: 8, core: 2. Of those that a mesh axis runs over, the one named last changes fastest.
Arguments:
- queries: bfloat16 [16384, 4096], P(('dp', 'ctx'), 'tp'), parts along dimension 0, may hold values from -1.5 to 1.5
- keys: bfloat16 [16384, 4096], P(('dp', 'ctx'), 'tp'), parts along dimension 0, may hold values from -1.5 to 1.5
- values: bfloat16 [16384, 8192], P(('dp', 'ctx'), 'tp'), parts along dimension 0, may hold values from -25 to 25
- gates: bfloat16 [16384, 8192], P(('dp', 'ctx'), 'tp'), parts along dimension 0, may hold values from -6 to 6
- decay_log: float32 [16, 16384], P('tp', ('dp', 'ctx')), parts along dimension 1, may hold values from -2.5 to 0
- out_weight: bfloat16 [8192, 4096], P('tp'), may hold values from -0.09375 to 0.09375
Outputs:
- mixed: bfloat16 [16384, 4096], P(('dp', 'ctx'), 'tp'), parts along dimension 0
There are 2 independent parts, one for each index of `dp`. A program takes and returns all parts, laid end to end along the dimension named above; an argument that names none is the same for every part. Nothing has to cross between parts.
All inputs are finite; a program needn't handle non-finite values.
Results may differ from a plain program's by a relative error of at most 0.0058.
Values may be sent and summed in bfloat16 or wider, within the bound.
A program may use at most 128 MiB of HBM per device.

v0:
```python
import jax
import jax.numpy as jnp
from jax import lax
from jax.sharding import PartitionSpec as P


def prefix(x, axis, combine, identity):
    count, place = (lax.axis_size(axis), lax.axis_index(axis))
    everything = jax.tree.map(lambda part: lax.all_gather(part, axis), x)
    start = jax.tree.map(
        lambda part, zero: jnp.broadcast_to(jnp.asarray(zero, part.dtype), part.shape), x, identity
    )

    def hop(k, before):
        reached = k < place
        new = combine(before, jax.tree.map(lambda part: part[k], everything))
        return jax.tree.map(lambda a, b: jnp.where(reached, a, b), new, before)

    return lax.fori_loop(0, count, hop, start)


def block_terms(query_heads, key_heads, value_per_head, decay_log):
    count = query_heads.shape[0]
    cumulative = jnp.cumsum(decay_log, axis=1)
    causal = lax.broadcasted_iota(jnp.int32, (count, count), 0) >= lax.broadcasted_iota(
        jnp.int32, (count, count), 1
    )
    spread = cumulative[:, :, None] - cumulative[:, None, :]
    decay_weight = jnp.exp(jnp.where(causal[None], spread, -1e30))
    scores = jnp.einsum("thd,shd->hts", query_heads, key_heads, preferred_element_type=jnp.float32)
    masked = (scores * decay_weight).astype(jnp.bfloat16)
    intra = jnp.einsum("hts,shv->thv", masked, value_per_head, preferred_element_type=jnp.float32)
    block_total = cumulative[:, -1]
    key_factor = jnp.exp(block_total[:, None] - cumulative).T
    decay_weighted_keys = (key_heads.astype(jnp.float32) * key_factor[:, :, None]).astype(
        jnp.bfloat16
    )
    block_state = jnp.einsum(
        "mcl,mcb->clb", decay_weighted_keys, value_per_head, preferred_element_type=jnp.float32
    )
    query_decayed = query_heads.astype(jnp.float32) * jnp.exp(cumulative).T[:, :, None]
    return (intra, query_decayed, block_state, block_total)


def chain_step(earlier, later):
    return (earlier[0] + later[0], jnp.exp(later[0])[:, None, None] * earlier[1] + later[1])


def body(queries, keys, values, gates, decay_log, out_weight):
    tok_count = queries.shape[0]
    heads_here = decay_log.shape[0]
    query_heads = queries.reshape(tok_count, heads_here, -1)
    key_heads = keys.reshape(tok_count, heads_here, -1)
    value_per_head = values.reshape(tok_count, heads_here, -1)
    intra, query_decayed, block_state, block_total = block_terms(
        query_heads, key_heads, value_per_head, decay_log
    )
    identity = (jnp.zeros_like(block_total), jnp.zeros_like(block_state))
    carried = prefix((block_total, block_state), "ctx", chain_step, identity)[1]
    cross = jnp.einsum(
        "zml,mli->zmi",
        query_decayed,
        carried,
        precision=lax.Precision.HIGHEST,
        preferred_element_type=jnp.float32,
    )
    retained = intra + cross
    normed = retained * lax.rsqrt(jnp.mean(retained * retained, axis=-1, keepdims=True) + 1e-06)
    gate_heads = gates.reshape(tok_count, heads_here, -1).astype(jnp.float32)
    gated = (jax.nn.silu(gate_heads) * normed).astype(jnp.bfloat16).reshape(tok_count, -1)
    partial_out = jnp.dot(gated, out_weight, preferred_element_type=jnp.float32)
    mixed = lax.psum_scatter(partial_out, "tp", scatter_dimension=1, tiled=True)
    return mixed.astype(jnp.bfloat16)


def solution(mesh):
    placed = (
        P(("dp", "ctx"), "tp"),
        P(("dp", "ctx"), "tp"),
        P(("dp", "ctx"), "tp"),
        P(("dp", "ctx"), "tp"),
        P("tp", ("dp", "ctx")),
        P("tp", None),
    )
    return jax.shard_map(
        body, mesh=mesh, in_specs=placed, out_specs=P(("dp", "ctx"), "tp"), check_vma=False
    )
```

profile of v0, /device:TPU:224, one launch (start us, length us, event | category | flops | bytes accessed | tf_op | source)
XLA Modules:
  0.0 226.5 jit_solution(12809022406121167044)
XLA Ops:
  6.5 0.0 copy-start
  6.5 0.0 all-gather.3.cloned.1.call-start
  6.5 1.1 reduce-window.6
  7.7 0.2 slice_reduce_fusion
  7.8 0.6 slice.12
  8.4 0.2 reduce-window.9
  8.6 0.1 fusion.22
  8.7 0.1 broadcast.48
  8.8 0.6 slice.13
  10.7 0.0 copy-done
  10.7 0.0 copy-start.3
  10.7 2.7 %fusion.16 = f32[256,512]{1,0:T(8,128)} fusion(bf16[1024,512]{1,0:T(8,128)(2,1)S(1)} %copy-done, bf16[1024,256]{1,0:T(8,128)(2,1)} %param.9, f32[1024]{0:T(1024)S(1)} %subtract_exponential_fusion), kind=kOutput, calls=%fused_computation.25 | convolution fusion | flops 269221888 | bytes 2101248 | tf_op jit(solution)/shard_map/mcl,mcb->clb/dot_general | solution.py:38
  13.3 0.0 all-gather.3.cloned.1.call-update
  13.4 0.0 reduce-scatter.2.cloned.1.call-start
  13.4 0.0 copy-done.5
  13.4 0.6 dynamic-slice
  14.0 0.6 bitcast_dynamic-update-slice_fusion
  14.7 14.0 %all-reduce = f32[8]{0:T(128)S(1)} all-reduce(f32[8]{0:T(128)S(1)} %bitcast_dynamic-update-slice_fusion), channel_id=1, replica_groups=mesh['dp'=2,'ctx'=8,'tp'=16] {'ctx'}, use_global_device_ids=true, to_apply=%add | all-reduce | flops 8 | bytes 64
  28.6 0.0 copy-done.1
  28.6 1.3 copy.9
  30.0 0.0 copy-done.3
  30.0 4.3 %fusion.8 = f32[1024,512]{0,1:T(8,128)} fusion(bf16[1024,512]{1,0:T(8,128)(2,1)S(1)} %copy-done, bf16[1024,256]{1,0:T(8,128)(2,1)S(1)} %copy-done.3, bf16[1024,256]{1,0:T(8,128)(2,1)} %param.9, f32[1024]{0:T(1024)S(1)} %get-tuple-element.139), kind=kOutput, calls=%fused_computation.17 | convolution fusion | flops 1615855616 | bytes 4198400 | tf_op jit(solution)/shard_map/hts,shv->thv/dot_general | solution.py:32
  34.2 32.6 %all-gather.3.cloned.1.call-done = f32[2048,512]{1,0:T(8,128)} async-done(((f32[256,512]{1,0:T(8,128)}), f32[2048,512]{1,0:T(8,128)}) %all-gather.3.cloned.1.call-update) | async-done | bytes 4194320 | tf_op jit(solution)/shard_map/all_gather | solution.py:9
  66.9 20.5 %while.14 = (s32[]{:T(128)}, f32[1,256,512]{2,1,0:T(8,128)S(1)}, s32[]{:T(128)}, f32[8,1]{0,1:T(1,128)S(1)}, f32[8,1,256,512]{3,2,1,0:T(8,128)}, /*index=5*/s32[]{:T(128)}, s32[]{:T(128)}) while((s32[]{:T(128)}, f32[1,256,512]{2,1,0:T(8,128)S(1)}, s32[]{:T(128)}, f32[8,1]{0,1:T(1,128)S(1)}, f32[8,1,256,512]{3,2,1,0:T(8,128)}, ...), condition=%wide.region_3.4_spmd.clone, body=%wide.region_2.3_spmd.clone.sunk | while | flops 524292 | bytes 1572989 | solution.py:19
  66.9 0.6 fusion.31
  67.5 1.9 fusion.32
  69.4 0.6 fusion.31
  70.0 1.9 fusion.32
  72.0 0.6 fusion.31
  72.6 1.9 fusion.32
  74.6 0.6 fusion.31
  75.2 1.9 fusion.32
  77.1 0.6 fusion.31
  77.7 1.9 fusion.32
  79.7 0.6 fusion.31
  80.3 1.9 fusion.32
  82.3 0.6 fusion.31
  82.9 1.9 fusion.32
  84.8 0.6 fusion.31
  85.4 1.9 fusion.32
  87.4 0.0 copy-start.2
  87.4 0.0 copy-start.4
  87.4 5.5 %fusion.7 = (f32[1024]{0:T(1024)S(1)}, f32[512,1024]{1,0:T(8,128)S(1)}) fusion(bf16[1024,256]{1,0:T(8,128)(2,1)S(1)} %copy-done.3, f32[1024]{0:T(1024)S(1)} %get-tuple-element.138, f32[1,256,512]{2,1,0:T(8,128)S(1)} %get-tuple-element.99, f32[1024,512]{0,1:T(8,128)} %fusion.8), kind=kOutput, calls=%fused_computation.15 | convolution fusion | flops 1612708864 | bytes 5251072 | tf_op jit(solution)/shard_map/zml,mli->zmi/dot_general | solution.py:60
  93.0 0.0 copy-done.2
  93.0 8.3 %fusion.10 = f32[1024,4096]{1,0:T(8,128)} fusion(bf16[512,4096]{1,0:T(8,128)(2,1)S(1)} %copy-done.4, f32[512,1024]{1,0:T(8,128)S(1)} %get-tuple-element.141, bf16[1024,512]{0,1:T(8,128)(2,1)S(1)} %copy-done.2, f32[1024]{0:T(1024)S(1)} %add_rsqrt_fusion), kind=kOutput, calls=%fused_computation.19 | convolution fusion | flops 4299161600 | bytes 24121344 | tf_op jit(solution)/shard_map/dot_general | solution.py:71
  101.3 0.0 reduce-scatter.2.cloned.1.call-update
  101.3 116.3 %reduce-scatter.2.cloned.1.call-done = f32[1024,256]{1,0:T(8,128)} async-done(((f32[1024,4096]{1,0:T(8,128)}), f32[1024,256]{1,0:T(8,128)}) %reduce-scatter.2.cloned.1.call-update) | async-done | bytes 1048592 | tf_op jit(solution)/shard_map/reduce_scatter | solution.py:72
  217.6 2.1 convert_element_type.32
  (8 shorter events, 0.0 us)
Async XLA Ops:
  6.5 4.1 %copy-start = (bf16[1024,512]{1,0:T(8,128)(2,1)S(1)}, bf16[1024,512]{1,0:T(8,128)(2,1)}, u32[]{:S(2)}) copy-start(bf16[1024,512]{1,0:T(8,128)(2,1)} %param.10) | copy-start | bytes 3145732
  6.5 6.9 %copy-start.5 = (u32[256]{0:T(256)S(1)}, u32[256]{0:T(256)}, u32[]{:S(2)}) copy-start(u32[256]{0:T(256)} %constant.49) | copy-start | bytes 3076
  6.5 22.1 %copy-start.1 = (bf16[1024,512]{1,0:T(8,128)(2,1)S(1)}, bf16[1024,512]{1,0:T(8,128)(2,1)}, u32[]{:S(2)}) copy-start(bf16[1024,512]{1,0:T(8,128)(2,1)} %param.11) | copy-start | bytes 3145732
  6.5 60.3 %all-gather.3.cloned.1.call-start = ((), (), s32[]{:S(2)}) async-start(), calls=%async_computation.2 | async-start | bytes 4718592 | tf_op jit(solution)/shard_map/all_gather | solution.py:9
  10.7 19.3 %copy-start.3 = (bf16[1024,256]{1,0:T(8,128)(2,1)S(1)}, bf16[1024,256]{1,0:T(8,128)(2,1)}, u32[]{:S(2)}) copy-start(bf16[1024,256]{1,0:T(8,128)(2,1)} %param.8) | copy-start | bytes 1572868
  13.4 204.3 %reduce-scatter.2.cloned.1.call-start = ((), (), s32[]{:S(2)}) async-start(), calls=%async_computation.1 | async-start | bytes 17825792 | tf_op jit(solution)/shard_map/reduce_scatter | solution.py:72
  87.4 5.6 %copy-start.2 = (bf16[1024,512]{0,1:T(8,128)(2,1)S(1)}, bf16[1024,512]{0,1:T(8,128)(2,1)}, u32[]{:S(2)}) copy-start(bf16[1024,512]{0,1:T(8,128)(2,1)} %copy.9) | copy-start | bytes 3145732
  87.4 5.6 %copy-start.4 = (bf16[512,4096]{1,0:T(8,128)(2,1)S(1)}, bf16[512,4096]{1,0:T(8,128)(2,1)}, u32[]{:S(2)}) copy-start(bf16[512,4096]{1,0:T(8,128)(2,1)} %param.13) | copy-start | bytes 12582916
Sparse Core Ops, SparseCore 0:
  13.5 53.3 all-gather.2
  101.5 116.1 reduce-scatter.1
where the time goes:
time: 230 us; the launch traced here: 227 us
  waiting for transfers between devices  149 us (65%)
  matrix products  20.8 us (9%)
  other arithmetic  19 us (8%)
  between operations  14.8 us (6%)
  blocking collectives  14 us (6%)
  local copies, waits for them, and re-layouts  8.8 us (4%)
    reduce_scatter x1, waiting for transfers between devices, body(): mixed = lax.psum_scatter(partial_out, 'tp', scatter_dimension=1, tiled=True)  116 us
    all_gather x1, waiting for transfers between devices, prefix(): everything = jax.tree.map(lambda part: lax.all_gather(part, axis), x)  32.6 us
    select_n x8, other arithmetic, hop(): return jax.tree.map(lambda a, b: jnp.where(reached, a, b), new, before)  15.6 us
    unnamed x1, blocking collectives  14 us
    dot_general x1, matrix products, body(): partial_out = jnp.dot(gated, out_weight, preferred_element_type=jnp.float32)  8.34 us
    dot_general x1, matrix products, body(): jnp.einsum('zml,mli->zmi', query_decayed, carried, precision=lax.Precisio...  5.52 us
    exp x8, local copies, waits for them, and re-layouts, chain_step(): jnp.exp(later[0])[:, None, None] * earlier[1] + later[1]  4.73 us
  transfers between devices with their start and end apart: 2, of which 2 were waited for; matrix products, arithmetic and copies ran while one was open for 3% of the time, Pallas kernels for 0%

commit v1 on v0

v1 whole, which is shorter than its diff:
```python
import jax
import jax.numpy as jnp
from jax import lax
from jax.experimental import pallas as pl
from jax.experimental.pallas import tpu as pltpu
from jax.sharding import PartitionSpec as P

MESH = pl.DeviceIdType.MESH
F32, BF16 = jnp.float32, jnp.bfloat16
SIDE = 4
BLOCK = 1024
DK, DV = 256, 512
COLS = 256
TILE = 256
TILES = BLOCK // TILE
CHUNKS = 8
ROWS = DK // CHUNKS


def dot(p, q, dims=((1,), (0,))):
    return lax.dot_general(p, q, (dims, ((), ())), preferred_element_type=F32)


def kernel(
    q_hbm, k_hbm, v_hbm, g_hbm, d_ref, w_hbm, o_ref,
    q, k, v, g, wg, col, state, carr, nxt, prob, ret, gat, part, come, own,
    ld, w_s, w_r, c_s, c_r, g_s, g_r, p_s, p_r,
):
    dp, z, tp = lax.axis_index("dp"), lax.axis_index("ctx"), lax.axis_index("tp")
    nz = lax.axis_size("ctx")
    y, x = tp // SIDE, tp % SIDE
    a = x + dp * (y - x)
    b = y + dp * (x - y)

    def place(a_, b_):
        return (1 - dp) * (SIDE * b_ + a_) + dp * (SIDE * a_ + b_)

    def a_peer(j):
        return (dp, z, place((a + j) % SIDE, b))

    def b_peer(j):
        return (dp, z, place(a, (b + j) % SIDE))

    def z_peer(j):
        return (dp, (z + j + nz) % nz, tp)

    barrier = pltpu.get_barrier_semaphore()
    for j in (1, 2, 3):
        pl.semaphore_signal(barrier, inc=1, device_id=a_peer(j), device_id_type=MESH)
        pl.semaphore_signal(barrier, inc=1, device_id=b_peer(j), device_id_type=MESH)
    for j in (1, -1):
        pl.semaphore_signal(barrier, inc=1, device_id=z_peer(j), device_id_type=MESH)

    loads = [
        pltpu.make_async_copy(src, dst, ld.at[i])
        for i, (src, dst) in enumerate(((k_hbm, k), (v_hbm, v), (q_hbm, q), (g_hbm, g)))
    ]
    for c in loads:
        c.start()
    a_rows = pl.ds(pl.multiple_of(a * DV, DV), DV)

    def w_cols(a_, c):
        return pl.ds(pl.multiple_of(place(a_, c) * COLS, COLS), COLS)

    own_w = [
        pltpu.make_async_copy(w_hbm.at[:, w_cols(a, c)], wg.at[c, a_rows], ld.at[4 + c])
        for c in range(SIDE)
    ]
    for c in own_w:
        c.start()
    pl.semaphore_wait(barrier, 8)

    def w_copy(j, c):
        return pltpu.make_async_remote_copy(
            src_ref=w_hbm.at[:, w_cols((a + j) % SIDE, c)], dst_ref=wg.at[c, a_rows],
            send_sem=w_s.at[j - 1, c], recv_sem=w_r.at[j - 1, c],
            device_id=a_peer(j), device_id_type=MESH,
        )

    for c in range(SIDE):
        for j in (2, 1, 3):
            w_copy(j, c).start()

    lane = lax.broadcasted_iota(jnp.int32, (8, 128), 1)
    run = jnp.concatenate([d_ref[:, 128 * r : 128 * (r + 1)] for r in range(8)], axis=0)
    for s in (1, 2, 4, 8, 16, 32, 64):
        run = run + jnp.where(lane >= s, pltpu.roll(run, s, 1), 0.0)
    rows, before = [], jnp.zeros((1, 1), F32)
    for r in range(8):
        rows.append(run[r : r + 1] + before)
        before = before + run[r : r + 1, 127:128]
    last = before
    turned = jnp.concatenate(rows + [jnp.zeros((120, 128), F32)], axis=0).T
    for r in range(8):
        col[128 * r : 128 * (r + 1), :] = turned[:, r : r + 1]
    cum_row = jnp.concatenate(rows, axis=1)

    loads[0].wait()
    loads[1].wait()
    weighted = (k[...].astype(F32) * jnp.exp(last - col[...])).astype(BF16)
    state[...] = dot(weighted, v[...], ((0,), (0,)))

    def c_copy(c):
        return pltpu.make_async_remote_copy(
            src_ref=nxt.at[pl.ds(c * ROWS, ROWS)], dst_ref=carr.at[pl.ds(c * ROWS, ROWS)],
            send_sem=c_s.at[c], recv_sem=c_r.at[c], device_id=z_peer(1), device_id_type=MESH,
        )

    @pl.when(z == 0)
    def _():
        nxt[...] = state[...].astype(BF16)
        for c in range(CHUNKS):
            c_copy(c).start()
        carr[...] = jnp.zeros_like(carr)

    loads[2].wait()
    t_at = lax.broadcasted_iota(jnp.int32, (TILE, TILE), 0)
    s_at = lax.broadcasted_iota(jnp.int32, (TILE, TILE), 1)
    for i in range(TILES):
        mine = slice(i * TILE, (i + 1) * TILE)
        for j in range(i + 1):
            theirs = slice(j * TILE, (j + 1) * TILE)
            spread = col[mine, :] - cum_row[:, theirs]
            if i == j:
                spread = jnp.where(t_at >= s_at, spread, -1e30)
            scores = dot(q[mine, :], k[theirs, :], ((1,), (1,)))
            prob[:, theirs] = (scores * jnp.exp(spread)).astype(BF16)
        upto = (i + 1) * TILE
        ret[mine, :] = dot(prob[:, :upto], v[:upto, :])

    @pl.when(z > 0)
    def _():
        fade = jnp.exp(last)
        for c in range(CHUNKS):
            at = slice(c * ROWS, (c + 1) * ROWS)
            c_copy(c).wait_recv()

            @pl.when(z < nz - 1)
            def _():
                nxt[at, :] = (fade * carr[at, :].astype(F32) + state[at, :]).astype(BF16)
                c_copy(c).start()

    loads[3].wait()

    def g_copy(i, j):
        here = gat.at[i, :, a_rows]
        return pltpu.make_async_remote_copy(
            src_ref=here, dst_ref=here, send_sem=g_s.at[i, j - 1], recv_sem=g_r.at[i, j - 1],
            device_id=a_peer(j), device_id_type=MESH,
        )

    def p_copy(i, j):
        return pltpu.make_async_remote_copy(
            src_ref=part.at[i, j - 1], dst_ref=come.at[i, j - 1],
            send_sem=p_s.at[i, j - 1], recv_sem=p_r.at[i, j - 1],
            device_id=b_peer(j), device_id_type=MESH,
        )

    @pl.loop(0, TILES)
    def _(i):
        at = pl.ds(pl.multiple_of(i * TILE, TILE), TILE)
        r = ret[at, :] + jnp.exp(col[at, :]) * dot(q[at, :], carr[...])
        r = r * lax.rsqrt(jnp.mean(r * r, axis=-1, keepdims=True) + 1e-6)
        u = g[at, :].astype(F32)
        gat[i, :, a_rows] = (u / (1.0 + jnp.exp(-u)) * r).astype(BF16)
        for j in (2, 1, 3):
            g_copy(i, j).start()

    for c in own_w:
        c.wait()
    for c in range(SIDE):
        for j in (1, 2, 3):
            w_copy(j, c).wait_recv()

    @pl.loop(0, TILES)
    def _(i):
        for j in (1, 2, 3):
            g_copy(i, j).wait_recv()
        heads = gat[i]
        for j in (2, 1, 3):
            part[i, j - 1] = dot(heads, wg[(b + j) % SIDE]).astype(BF16)
            p_copy(i, j).start()
        own[i] = dot(heads, wg[b])

    @pl.loop(0, TILES)
    def _(i):
        for j in (1, 2, 3):
            p_copy(i, j).wait_recv()
        total = own[i]
        for j in (1, 2, 3):
            total = total + come[i, j - 1].astype(F32)
        o_ref[pl.ds(pl.multiple_of(i * TILE, TILE), TILE), :] = total.astype(BF16)

    for c in range(SIDE):
        for j in (1, 2, 3):
            w_copy(j, c).wait_send()

    @pl.when(z < nz - 1)
    def _():
        for c in range(CHUNKS):
            c_copy(c).wait_send()

    @pl.loop(0, TILES)
    def _(i):
        for j in (1, 2, 3):
            g_copy(i, j).wait_send()
            p_copy(i, j).wait_send()


def layer(queries, keys, values, gates, decay_log, out_weight):
    dma = pltpu.SemaphoreType.DMA
    anywhere = pl.BlockSpec(memory_space=pl.ANY)
    vmem = pl.BlockSpec(memory_space=pltpu.VMEM)
    return pl.pallas_call(
        kernel,
        out_shape=jax.ShapeDtypeStruct((BLOCK, COLS), BF16),
        in_specs=[anywhere] * 4 + [vmem, anywhere],
        out_specs=vmem,
        scratch_shapes=[
            pltpu.VMEM((BLOCK, DK), BF16),
            pltpu.VMEM((BLOCK, DK), BF16),
            pltpu.VMEM((BLOCK, DV), BF16),
            pltpu.VMEM((BLOCK, DV), BF16),
            pltpu.VMEM((SIDE, SIDE * DV, COLS), BF16),
            pltpu.VMEM((BLOCK, 1), F32),
            pltpu.VMEM((DK, DV), F32),
            pltpu.VMEM((DK, DV), BF16),
            pltpu.VMEM((DK, DV), BF16),
            pltpu.VMEM((TILE, BLOCK), BF16),
            pltpu.VMEM((BLOCK, DV), F32),
            pltpu.VMEM((TILES, TILE, SIDE * DV), BF16),
            pltpu.VMEM((TILES, 3, TILE, COLS), BF16),
            pltpu.VMEM((TILES, 3, TILE, COLS), BF16),
            pltpu.VMEM((TILES, TILE, COLS), F32),
            dma((8,)),
            dma((3, SIDE)), dma((3, SIDE)),
            dma((CHUNKS,)), dma((CHUNKS,)),
            dma((TILES, 3)), dma((TILES, 3)),
            dma((TILES, 3)), dma((TILES, 3)),
        ],
        compiler_params=pltpu.CompilerParams(
            collective_id=0, has_side_effects=True, vmem_limit_bytes=48 * 2**20
        ),
        cost_estimate=pl.CostEstimate(
            flops=7 * 10**9, bytes_accessed=8 * 2**20, transcendentals=2 * 2**20
        ),
        name="retention",
    )(queries, keys, values, gates, decay_log, out_weight)


def solution(mesh):
    rows = P(("dp", "ctx"), "tp")
    placed = (rows, rows, rows, rows, P("tp", ("dp", "ctx")), P("tp", None))
    return jax.shard_map(layer, mesh=mesh, in_specs=placed, out_specs=rows, check_vma=False)
```

time: 230 us -> 83.2 us (0.36); the launches traced: 227 us -> 82.9 us
  waiting for transfers between devices: 149 us -> 0 us
  Pallas kernels: 0 us -> 76.9 us
  matrix products: 20.8 us -> 0 us
  other arithmetic: 19 us -> 0 us
  between operations: 14.8 us -> 0.01 us
  blocking collectives: 14 us -> 0 us
  local copies, waits for them, and re-layouts: 8.8 us -> 6.01 us
    reduce_scatter x1 -> x0, waiting for transfers between devices: 116 us -> none  [body(): mixed = lax.psum_scatter(partial_out, 'tp', scatter_dimension=1, tiled=True)]
    pallas_call x0 -> x1, Pallas kernels: none -> 76.9 us  [layer(): pl.pallas_call(kernel, out_shape=jax.ShapeDtypeStruct((BLOCK, COLS), BF16...]
    all_gather x1 -> x0, waiting for transfers between devices: 32.6 us -> none  [prefix(): everything = jax.tree.map(lambda part: lax.all_gather(part, axis), x)]
    dot_general x4 -> x0, matrix products: 20.8 us -> none  [the longest x1 8.34 us: body(): partial_out = jnp.dot(gated, out_weight, preferred_element_type=jnp.float32)]
    select_n x8 -> x0, other arithmetic: 15.6 us -> none  [hop(): return jax.tree.map(lambda a, b: jnp.where(reached, a, b), new, before)]
    unnamed x1 -> x0, blocking collectives: 14 us -> none
    exp x8 -> x0, local copies, waits for them, and re-layouts: 4.73 us -> none  [chain_step(): jnp.exp(later[0])[:, None, None] * earlier[1] + later[1]]
    unnamed x16 -> x11, local copies, waits for them, and re-layouts: 2.61 us -> 6.01 us
  transfers between devices with their start and end apart: 2 -> 0, of which waited for: 2 -> 0; matrix products, arithmetic and copies ran while one was open for 3% -> 0% of each run, Pallas kernels for 0% -> 0%
where the time goes in v1:
time: 83.2 us; the launch traced here: 82.9 us
  Pallas kernels  76.9 us (92%)
  local copies, waits for them, and re-layouts  6.01 us (7%)
    pallas_call x1, Pallas kernels, layer(): pl.pallas_call(kernel, out_shape=jax.ShapeDtypeStruct((BLOCK, COLS), BF16...  76.9 us
    unnamed x11, local copies, waits for them, and re-layouts  6.01 us

profile of v1, /device:TPU:224, one launch (start us, length us, event | category | flops | bytes accessed | tf_op | source)
XLA Modules:
  0.0 82.9 jit_solution(9882224419687059561)
XLA Ops:
  0.0 0.0 copy-start
  0.0 1.2 %copy-done = bf16[1024,512]{1,0:T(8,128)(2,1)S(1)} copy-done((bf16[1024,512]{1,0:T(8,128)(2,1)S(1)}, bf16[1024,512]{1,0:T(8,128)(2,1)}, u32[]{:S(2)}) %copy-start) | copy-done | bytes 1048600
  1.2 0.0 copy-start.1
  1.2 1.2 %copy-done.1 = bf16[1024,512]{1,0:T(8,128)(2,1)S(1)} copy-done((bf16[1024,512]{1,0:T(8,128)(2,1)S(1)}, bf16[1024,512]{1,0:T(8,128)(2,1)}, u32[]{:S(2)}) %copy-start.1) | copy-done | bytes 1048600
  2.5 0.0 copy-start.2
  2.5 1.0 %copy-done.2 = bf16[1024,256]{1,0:T(8,128)(2,1)S(1)} copy-done((bf16[1024,256]{1,0:T(8,128)(2,1)S(1)}, bf16[1024,256]{1,0:T(8,128)(2,1)}, u32[]{:S(2)}) %copy-start.2) | copy-done | bytes 524312
  3.5 0.0 copy-start.3
  3.5 1.0 %copy-done.3 = bf16[1024,256]{1,0:T(8,128)(2,1)S(1)} copy-done((bf16[1024,256]{1,0:T(8,128)(2,1)S(1)}, bf16[1024,256]{1,0:T(8,128)(2,1)}, u32[]{:S(2)}) %copy-start.3) | copy-done | bytes 524312
  4.5 0.0 copy-start.4
  4.5 0.7 copy-done.4
  5.2 76.9 %retention.1 = bf16[1024,256]{1,0:T(8,128)(2,1)S(1)} custom-call(bf16[1024,256]{1,0:T(8,128)(2,1)S(1)} %copy-done.2, bf16[1024,256]{1,0:T(8,128)(2,1)S(1)} %copy-done.3, bf16[1024,512]{1,0:T(8,128)(2,1)S(1)} %copy-done, bf16[1024,512]{1,0:T(8,128)(2,1)S(1)} %copy-done.1, f32[1,1024]{1,0:T(1,128)S(1)} %copy-done.4, bf16[512,4096]{1,0:T(8,128)(2,1)} %w_hbm.1), custom_call_target="tpu_custom_call" | custom-call | flops 7000000000 | bytes 8388608 | tf_op jit(solution)/shard_map/retention/pallas_call | solution.py:214
  82.1 0.8 copy.8
Async XLA Ops:
  0.0 1.2 %copy-start = (bf16[1024,512]{1,0:T(8,128)(2,1)S(1)}, bf16[1024,512]{1,0:T(8,128)(2,1)}, u32[]{:S(2)}) copy-start(bf16[1024,512]{1,0:T(8,128)(2,1)} %v_hbm.1) | copy-start | bytes 3145732
  1.2 1.2 %copy-start.1 = (bf16[1024,512]{1,0:T(8,128)(2,1)S(1)}, bf16[1024,512]{1,0:T(8,128)(2,1)}, u32[]{:S(2)}) copy-start(bf16[1024,512]{1,0:T(8,128)(2,1)} %g_hbm.1) | copy-start | bytes 3145732
  2.5 1.0 %copy-start.2 = (bf16[1024,256]{1,0:T(8,128)(2,1)S(1)}, bf16[1024,256]{1,0:T(8,128)(2,1)}, u32[]{:S(2)}) copy-start(bf16[1024,256]{1,0:T(8,128)(2,1)} %q_hbm.1) | copy-start | bytes 1572868
  3.5 1.0 %copy-start.3 = (bf16[1024,256]{1,0:T(8,128)(2,1)S(1)}, bf16[1024,256]{1,0:T(8,128)(2,1)}, u32[]{:S(2)}) copy-start(bf16[1024,256]{1,0:T(8,128)(2,1)} %k_hbm.1) | copy-start | bytes 1572868
  4.5 0.7 copy-start.4

commit v2 on v1

--- a/solution.py
+++ b/solution.py
@@ -24,7 +24,7 @@
 def kernel(
     q_hbm, k_hbm, v_hbm, g_hbm, d_ref, w_hbm, o_ref,
     q, k, v, g, wg, col, state, carr, nxt, prob, ret, gat, part, come, own,
-    ld, w_s, w_r, c_s, c_r, g_s, g_r, p_s, p_r,
+    ld, w_s, w_r, c_s, c_r, g_s, g_r, f_s, f_r, p_s, p_r,
 ):
     dp, z, tp = lax.axis_index("dp"), lax.axis_index("ctx"), lax.axis_index("tp")
     nz = lax.axis_size("ctx")
@@ -145,9 +145,22 @@
     def g_copy(i, j):
         here = gat.at[i, :, a_rows]
         return pltpu.make_async_remote_copy(
-            src_ref=here, dst_ref=here, send_sem=g_s.at[i, j - 1], recv_sem=g_r.at[i, j - 1],
+            src_ref=here, dst_ref=here, send_sem=g_s.at[i, j // 2], recv_sem=g_r.at[i, j // 2],
             device_id=a_peer(j), device_id_type=MESH,
         )
+
+    def f_copy(i, j):
+        cols = pl.ds(pl.multiple_of((a + 4 - j) % SIDE * DV, DV), DV)
+        here = gat.at[i, pl.ds(j // 2 * (TILE // 2), TILE // 2), cols]
+        return pltpu.make_async_remote_copy(
+            src_ref=here, dst_ref=here, send_sem=f_s.at[i, j // 2], recv_sem=f_r.at[i, j // 2],
+            device_id=a_peer(j), device_id_type=MESH,
+        )
+
+    def pass_on(i):
+        for j in (1, 3):
+            g_copy(i, j).wait_recv()
+            f_copy(i, j).start()
 
     def p_copy(i, j):
         return pltpu.make_async_remote_copy(
@@ -163,7 +176,7 @@
         r = r * lax.rsqrt(jnp.mean(r * r, axis=-1, keepdims=True) + 1e-6)
         u = g[at, :].astype(F32)
         gat[i, :, a_rows] = (u / (1.0 + jnp.exp(-u)) * r).astype(BF16)
-        for j in (2, 1, 3):
+        for j in (1, 3):
             g_copy(i, j).start()
 
     for c in own_w:
@@ -172,10 +185,16 @@
         for j in (1, 2, 3):
             w_copy(j, c).wait_recv()
 
-    @pl.loop(0, TILES)
-    def _(i):
-        for j in (1, 2, 3):
-            g_copy(i, j).wait_recv()
+    pass_on(0)
+
+    @pl.loop(0, TILES)
+    def _(i):
+        @pl.when(i < TILES - 1)
+        def _():
+            pass_on(i + 1)
+
+        for j in (1, 3):
+            f_copy(i, j).wait_recv()
         heads = gat[i]
         for j in (2, 1, 3):
             part[i, j - 1] = dot(heads, wg[(b + j) % SIDE]).astype(BF16)
@@ -202,8 +221,10 @@
 
     @pl.loop(0, TILES)
     def _(i):
-        for j in (1, 2, 3):
+        for j in (1, 3):
             g_copy(i, j).wait_send()
+            f_copy(i, j).wait_send()
+        for j in (1, 2, 3):
             p_copy(i, j).wait_send()
 
 
@@ -235,11 +256,12 @@
             dma((8,)),
             dma((3, SIDE)), dma((3, SIDE)),
             dma((CHUNKS,)), dma((CHUNKS,)),
-            dma((TILES, 3)), dma((TILES, 3)),
+            dma((TILES, 2)), dma((TILES, 2)),
+            dma((TILES, 2)), dma((TILES, 2)),
             dma((TILES, 3)), dma((TILES, 3)),
         ],
         compiler_params=pltpu.CompilerParams(
-            collective_id=0, has_side_effects=True, vmem_limit_bytes=48 * 2**20
+            collective_id=0, has_side_effects=True, vmem_limit_bytes=60 * 2**20
         ),
         cost_estimate=pl.CostEstimate(
             flops=7 * 10**9, bytes_accessed=8 * 2**20, transcendentals=2 * 2**20

time: 83.2 us -> 74.5 us (0.90)
  Pallas kernels: 76.9 us -> 72.4 us
  local copies, waits for them, and re-layouts: 6.01 us -> 1.87 us
    pallas_call x1, Pallas kernels: 76.9 us -> 72.4 us  [layer(): pl.pallas_call(kernel, out_shape=jax.ShapeDtypeStruct((BLOCK, COLS), BF16...]
    unnamed x11 -> x1, local copies, waits for them, and re-layouts: 6.01 us -> 1.87 us
where the time goes in v2:
time: 74.5 us; the launch traced here: 74.3 us
  Pallas kernels  72.4 us (97%)
  local copies, waits for them, and re-layouts  1.87 us (3%)
    pallas_call x1, Pallas kernels, layer(): pl.pallas_call(kernel, out_shape=jax.ShapeDtypeStruct((BLOCK, COLS), BF16...  72.4 us
    unnamed x1, local copies, waits for them, and re-layouts  1.87 us

profile of v2, /device:TPU:224, one launch (start us, length us, event | category | flops | bytes accessed | tf_op | source)
XLA Modules:
  0.0 74.3 jit_solution(3407742930463137344)
XLA Ops:
  0.0 72.4 %retention.1 = bf16[1024,256]{1,0:T(8,128)(2,1)} custom-call(bf16[1024,256]{1,0:T(8,128)(2,1)} %q_hbm.1, bf16[1024,256]{1,0:T(8,128)(2,1)} %k_hbm.1, bf16[1024,512]{1,0:T(8,128)(2,1)} %v_hbm.1, bf16[1024,512]{1,0:T(8,128)(2,1)} %g_hbm.1, f32[1,1024]{1,0:T(1,128)} %d_ref.1, bf16[512,4096]{1,0:T(8,128)(2,1)} %w_hbm.1), custom_call_target="tpu_custom_call" | custom-call | flops 7000000000 | bytes 8388608 | tf_op jit(solution)/shard_map/retention/pallas_call | solution.py:235
  72.4 1.9 %copy.8 = bf16[1024,256]{1,0:T(8,128)(2,1)} copy(bf16[1024,256]{1,0:T(8,128)(2,1)} %retention.1) | data formatting | bytes 1048576

commit v3 on v2

--- a/solution.py
+++ b/solution.py
@@ -13,7 +13,8 @@
 COLS = 256
 TILE = 256
 TILES = BLOCK // TILE
-CHUNKS = 8
+AHEAD = 2
+CHUNKS = 16
 ROWS = DK // CHUNKS
 
 
@@ -23,8 +24,8 @@
 
 def kernel(
     q_hbm, k_hbm, v_hbm, g_hbm, d_ref, w_hbm, o_ref,
-    q, k, v, g, wg, col, state, carr, nxt, prob, ret, gat, part, come, own,
-    ld, w_s, w_r, c_s, c_r, g_s, g_r, f_s, f_r, p_s, p_r,
+    q, k, v, g, wg, col, state, into, out, tell, told, prob, ret, gat, part, come, own,
+    ld, w_s, w_r, c_s, c_r, t_s, t_r, g_s, g_r, f_s, f_r, p_s, p_r,
 ):
     dp, z, tp = lax.axis_index("dp"), lax.axis_index("ctx"), lax.axis_index("tp")
     nz = lax.axis_size("ctx")
@@ -100,18 +101,71 @@
     weighted = (k[...].astype(F32) * jnp.exp(last - col[...])).astype(BF16)
     state[...] = dot(weighted, v[...], ((0,), (0,)))
 
-    def c_copy(c):
-        return pltpu.make_async_remote_copy(
-            src_ref=nxt.at[pl.ds(c * ROWS, ROWS)], dst_ref=carr.at[pl.ds(c * ROWS, ROWS)],
-            send_sem=c_s.at[c], recv_sem=c_r.at[c], device_id=z_peer(1), device_id_type=MESH,
-        )
+    fade = jnp.exp(last)
+
+    def chunk(c):
+        return pl.ds(pl.multiple_of(c * ROWS, ROWS), ROWS)
+
+    def c_copy(s, c, passing=False):
+        src = into if passing else out
+        return pltpu.make_async_remote_copy(
+            src_ref=src.at[s, chunk(c)], dst_ref=into.at[s, chunk(c)],
+            send_sem=c_s.at[s, c], recv_sem=c_r.at[s, c],
+            device_id=z_peer(-1 if s == 2 else 1), device_id_type=MESH,
+        )
+
+    def w_tell(s):
+        return pltpu.make_async_remote_copy(
+            src_ref=tell.at[s], dst_ref=told.at[s], send_sem=t_s.at[s], recv_sem=t_r.at[s],
+            device_id=z_peer(-1 if s == 2 else 1), device_id_type=MESH,
+        )
+
+    def source(s):
+        if s:
+            tell[s] = jnp.broadcast_to(fade, (8, 128))
+            w_tell(s).start()
+        out[s] = state[...].astype(BF16)
+        for c in range(CHUNKS):
+            c_copy(s, c).start()
+
+    def relay(s):
+        if s:
+            w_tell(s).wait_recv()
+            tell[s] = told[s] * fade
+
+            @pl.when(z > 0)
+            def _():
+                w_tell(s).start()
+
+        scale = told[2, 0:1, 0:1] if s == 2 else fade
+
+        @pl.loop(0, CHUNKS)
+        def _(c):
+            c_copy(s, c).wait_recv()
+            came, held = into[s, chunk(c), :].astype(F32), state[chunk(c), :]
+            new = came + scale * held if s == 2 else scale * came + held
+            out[s, chunk(c), :] = new.astype(BF16)
+            c_copy(s, c).start()
+
+    def accept(s):
+        for c in range(CHUNKS):
+            c_copy(s, c).wait_recv()
+
+    def join():
+        into[0] = (into[1].astype(F32) + told[1, 0:1, 0:1] * into[2].astype(F32)).astype(BF16)
 
     @pl.when(z == 0)
     def _():
-        nxt[...] = state[...].astype(BF16)
-        for c in range(CHUNKS):
-            c_copy(c).start()
-        carr[...] = jnp.zeros_like(carr)
+        source(0)
+        into[0] = jnp.zeros((DK, DV), BF16)
+
+    @pl.when(z == 4)
+    def _():
+        source(1)
+
+    @pl.when(z == 3)
+    def _():
+        source(2)
 
     loads[2].wait()
     t_at = lax.broadcasted_iota(jnp.int32, (TILE, TILE), 0)
@@ -128,17 +182,41 @@
         upto = (i + 1) * TILE
         ret[mine, :] = dot(prob[:, :upto], v[:upto, :])
 
-    @pl.when(z > 0)
-    def _():
-        fade = jnp.exp(last)
-        for c in range(CHUNKS):
-            at = slice(c * ROWS, (c + 1) * ROWS)
-            c_copy(c).wait_recv()
-
-            @pl.when(z < nz - 1)
-            def _():
-                nxt[at, :] = (fade * carr[at, :].astype(F32) + state[at, :]).astype(BF16)
-                c_copy(c).start()
+    @pl.when(z == 2)
+    def _():
+        relay(2)
+
+    @pl.when((z == 5) | (z == 6))
+    def _():
+        relay(1)
+
+    @pl.when((z >= 1) & (z <= 4))
+    def _():
+        relay(0)
+
+    @pl.when(z <= 1)
+    def _():
+        relay(2)
+
+    @pl.when(z == 5)
+    def _():
+        accept(0)
+
+    @pl.when(z == 6)
+    def _():
+        accept(2)
+        join()
+
+    @pl.when(z == 7)
+    def _():
+        @pl.loop(0, CHUNKS)
+        def _(c):
+            c_copy(2, c).wait_recv()
+            c_copy(2, c, True).start()
+
+        w_tell(1).wait_recv()
+        accept(1)
+        join()
 
     loads[3].wait()
 
@@ -169,30 +247,16 @@
             device_id=b_peer(j), device_id_type=MESH,
         )
 
-    @pl.loop(0, TILES)
-    def _(i):
+    def gate(i):
         at = pl.ds(pl.multiple_of(i * TILE, TILE), TILE)
-        r = ret[at, :] + jnp.exp(col[at, :]) * dot(q[at, :], carr[...])
+        r = ret[at, :] + jnp.exp(col[at, :]) * dot(q[at, :], into[0])
         r = r * lax.rsqrt(jnp.mean(r * r, axis=-1, keepdims=True) + 1e-6)
         u = g[at, :].astype(F32)
         gat[i, :, a_rows] = (u / (1.0 + jnp.exp(-u)) * r).astype(BF16)
         for j in (1, 3):
             g_copy(i, j).start()
 
-    for c in own_w:
-        c.wait()
-    for c in range(SIDE):
-        for j in (1, 2, 3):
-            w_copy(j, c).wait_recv()
-
-    pass_on(0)
-
-    @pl.loop(0, TILES)
-    def _(i):
-        @pl.when(i < TILES - 1)
-        def _():
-            pass_on(i + 1)
-
+    def project(i):
         for j in (1, 3):
             f_copy(i, j).wait_recv()
         heads = gat[i]
@@ -200,6 +264,32 @@
             part[i, j - 1] = dot(heads, wg[(b + j) % SIDE]).astype(BF16)
             p_copy(i, j).start()
         own[i] = dot(heads, wg[b])
+
+    @pl.loop(0, AHEAD)
+    def _(i):
+        gate(i)
+
+    @pl.loop(0, TILES + 1)
+    def _(i):
+        @pl.when(i < TILES)
+        def _():
+            pass_on(i)
+
+        @pl.when(i + AHEAD < TILES)
+        def _():
+            gate(i + AHEAD)
+
+        @pl.when(i == 1)
+        def _():
+            for c in own_w:
+                c.wait()
+            for c in range(SIDE):
+                for j in (1, 2, 3):
+                    w_copy(j, c).wait_recv()
+
+        @pl.when(i > 0)
+        def _():
+            project(i - 1)
 
     @pl.loop(0, TILES)
     def _(i):
@@ -214,10 +304,26 @@
         for j in (1, 2, 3):
             w_copy(j, c).wait_send()
 
-    @pl.when(z < nz - 1)
-    def _():
+    def sent(s):
         for c in range(CHUNKS):
-            c_copy(c).wait_send()
+            c_copy(s, c).wait_send()
+
+    @pl.when(z <= 4)
+    def _():
+        sent(0)
+
+    @pl.when((z >= 4) & (z <= 6))
+    def _():
+        sent(1)
+        w_tell(1).wait_send()
+
+    @pl.when((z <= 3) | (z == 7))
+    def _():
+        sent(2)
+
+    @pl.when((z >= 1) & (z <= 3))
+    def _():
+        w_tell(2).wait_send()
 
     @pl.loop(0, TILES)
     def _(i):
@@ -245,8 +351,10 @@
             pltpu.VMEM((SIDE, SIDE * DV, COLS), BF16),
             pltpu.VMEM((BLOCK, 1), F32),
             pltpu.VMEM((DK, DV), F32),
-            pltpu.VMEM((DK, DV), BF16),
-            pltpu.VMEM((DK, DV), BF16),
+            pltpu.VMEM((3, DK, DV), BF16),
+            pltpu.VMEM((3, DK, DV), BF16),
+            pltpu.VMEM((3, 8, 128), F32),
+            pltpu.VMEM((3, 8, 128), F32),
             pltpu.VMEM((TILE, BLOCK), BF16),
             pltpu.VMEM((BLOCK, DV), F32),
             pltpu.VMEM((TILES, TILE, SIDE * DV), BF16),
@@ -255,7 +363,8 @@
             pltpu.VMEM((TILES, TILE, COLS), F32),
             dma((8,)),
             dma((3, SIDE)), dma((3, SIDE)),
-            dma((CHUNKS,)), dma((CHUNKS,)),
+            dma((3, CHUNKS)), dma((3, CHUNKS)),
+            dma((3,)), dma((3,)),
             dma((TILES, 2)), dma((TILES, 2)),
             dma((TILES, 2)), dma((TILES, 2)),
             dma((TILES, 3)), dma((TILES, 3)),

time: 74.5 us -> 73.6 us (0.988)
  the two profiles are of different devices: /device:TPU:224 before, /device:TPU:6 now
where the time goes in v3:
time: 73.6 us; the launch traced here: 73.5 us
  Pallas kernels  71.6 us (97%)
  local copies, waits for them, and re-layouts  1.87 us (3%)
    pallas_call x1, Pallas kernels, layer(): pl.pallas_call(kernel, out_shape=jax.ShapeDtypeStruct((BLOCK, COLS), BF16...  71.6 us
    unnamed x1, local copies, waits for them, and re-layouts  1.87 us

profile of v3, /device:TPU:6, one launch (start us, length us, event | category | flops | bytes accessed | tf_op | source)
XLA Modules:
  0.0 73.5 jit_solution(1503744316321216195)
XLA Ops:
  0.0 71.6 %retention.1 = bf16[1024,256]{1,0:T(8,128)(2,1)} custom-call(bf16[1024,256]{1,0:T(8,128)(2,1)} %q_hbm.1, bf16[1024,256]{1,0:T(8,128)(2,1)} %k_hbm.1, bf16[1024,512]{1,0:T(8,128)(2,1)} %v_hbm.1, bf16[1024,512]{1,0:T(8,128)(2,1)} %g_hbm.1, f32[1,1024]{1,0:T(1,128)} %d_ref.1, bf16[512,4096]{1,0:T(8,128)(2,1)} %w_hbm.1), custom_call_target="tpu_custom_call" | custom-call | flops 7000000000 | bytes 8388608 | tf_op jit(solution)/shard_map/retention/pallas_call | solution.py:341
  71.6 1.9 %copy.8 = bf16[1024,256]{1,0:T(8,128)(2,1)} copy(bf16[1024,256]{1,0:T(8,128)(2,1)} %retention.1) | data formatting | bytes 1048576

commit v4 on v3

--- a/solution.py
+++ b/solution.py
@@ -25,7 +25,7 @@
 def kernel(
     q_hbm, k_hbm, v_hbm, g_hbm, d_ref, w_hbm, o_ref,
     q, k, v, g, wg, col, state, into, out, tell, told, prob, ret, gat, part, come, own,
-    ld, w_s, w_r, c_s, c_r, t_s, t_r, g_s, g_r, f_s, f_r, p_s, p_r,
+    ld, w_s, w_r, x_s, x_r, c_s, c_r, t_s, t_r, g_s, g_r, f_s, f_r, p_s, p_r,
 ):
     dp, z, tp = lax.axis_index("dp"), lax.axis_index("ctx"), lax.axis_index("tp")
     nz = lax.axis_size("ctx")
@@ -69,18 +69,31 @@
     ]
     for c in own_w:
         c.start()
-    pl.semaphore_wait(barrier, 8)
-
-    def w_copy(j, c):
-        return pltpu.make_async_remote_copy(
-            src_ref=w_hbm.at[:, w_cols((a + j) % SIDE, c)], dst_ref=wg.at[c, a_rows],
-            send_sem=w_s.at[j - 1, c], recv_sem=w_r.at[j - 1, c],
+    parity = z % 2
+    order = [(j, c) for c in (0, 1) for j in (2, 1, 3)]
+
+    def w_copy(j, c, other=False):
+        c_ = 2 * (1 - parity if other else parity) + c
+        return pltpu.make_async_remote_copy(
+            src_ref=w_hbm.at[:, w_cols((a + j) % SIDE, c_)], dst_ref=wg.at[c_, a_rows],
+            send_sem=w_s.at[int(other), j - 1, c], recv_sem=w_r.at[int(other), j - 1, c],
             device_id=a_peer(j), device_id_type=MESH,
         )
 
-    for c in range(SIDE):
-        for j in (2, 1, 3):
-            w_copy(j, c).start()
+    def x_copy(u, j, c, coming=False):
+        c_ = 2 * (1 - parity if coming else parity) + c
+        half = (a + SIDE - j) % SIDE * DV + u * (DV // 2)
+        here = wg.at[c_, pl.ds(pl.multiple_of(half, DV // 2), DV // 2)]
+        return pltpu.make_async_remote_copy(
+            src_ref=here, dst_ref=here, send_sem=x_s.at[u, j - 1, c], recv_sem=x_r.at[u, j - 1, c],
+            device_id=z_peer(1 - 2 * u), device_id_type=MESH,
+        )
+
+    def share(halves):
+        for j, c in order:
+            w_copy(j, c).wait_recv()
+            for u in halves:
+                x_copy(u, j, c).start()
 
     lane = lax.broadcasted_iota(jnp.int32, (8, 128), 1)
     run = jnp.concatenate([d_ref[:, 128 * r : 128 * (r + 1)] for r in range(8)], axis=0)
@@ -154,6 +167,8 @@
     def join():
         into[0] = (into[1].astype(F32) + told[1, 0:1, 0:1] * into[2].astype(F32)).astype(BF16)
 
+    pl.semaphore_wait(barrier, 8)
+
     @pl.when(z == 0)
     def _():
         source(0)
@@ -166,6 +181,14 @@
     @pl.when(z == 3)
     def _():
         source(2)
+
+    for j, c in order:
+        w_copy(j, c).start()
+
+    @pl.when(z >= 4)
+    def _():
+        for j, c in order:
+            w_copy(j, c, True).start()
 
     loads[2].wait()
     t_at = lax.broadcasted_iota(jnp.int32, (TILE, TILE), 0)
@@ -182,42 +205,6 @@
         upto = (i + 1) * TILE
         ret[mine, :] = dot(prob[:, :upto], v[:upto, :])
 
-    @pl.when(z == 2)
-    def _():
-        relay(2)
-
-    @pl.when((z == 5) | (z == 6))
-    def _():
-        relay(1)
-
-    @pl.when((z >= 1) & (z <= 4))
-    def _():
-        relay(0)
-
-    @pl.when(z <= 1)
-    def _():
-        relay(2)
-
-    @pl.when(z == 5)
-    def _():
-        accept(0)
-
-    @pl.when(z == 6)
-    def _():
-        accept(2)
-        join()
-
-    @pl.when(z == 7)
-    def _():
-        @pl.loop(0, CHUNKS)
-        def _(c):
-            c_copy(2, c).wait_recv()
-            c_copy(2, c, True).start()
-
-        w_tell(1).wait_recv()
-        accept(1)
-        join()
-
     loads[3].wait()
 
     def g_copy(i, j):
@@ -239,13 +226,6 @@
         for j in (1, 3):
             g_copy(i, j).wait_recv()
             f_copy(i, j).start()
-
-    def p_copy(i, j):
-        return pltpu.make_async_remote_copy(
-            src_ref=part.at[i, j - 1], dst_ref=come.at[i, j - 1],
-            send_sem=p_s.at[i, j - 1], recv_sem=p_r.at[i, j - 1],
-            device_id=b_peer(j), device_id_type=MESH,
-        )
 
     def gate(i):
         at = pl.ds(pl.multiple_of(i * TILE, TILE), TILE)
@@ -256,6 +236,74 @@
         for j in (1, 3):
             g_copy(i, j).start()
 
+    def start_gates():
+        @pl.loop(0, AHEAD)
+        def _(i):
+            gate(i)
+
+    @pl.when(z == 2)
+    def _():
+        relay(2)
+
+    @pl.when((z == 5) | (z == 6))
+    def _():
+        relay(1)
+
+    @pl.when(z == 0)
+    def _():
+        start_gates()
+
+    @pl.when(z == 7)
+    def _():
+        share((0,))
+
+    @pl.when((z >= 1) & (z <= 4))
+    def _():
+        relay(0)
+
+    @pl.when(z <= 1)
+    def _():
+        relay(2)
+
+    @pl.when(z == 0)
+    def _():
+        share((0,))
+
+    @pl.when((z == 1) | (z == 2))
+    def _():
+        share((0, 1))
+
+    @pl.when((z == 3) | (z == 4))
+    def _():
+        share((1,))
+
+    @pl.when(z == 5)
+    def _():
+        accept(0)
+
+    @pl.when(z == 6)
+    def _():
+        accept(2)
+        join()
+
+    @pl.when(z == 7)
+    def _():
+        @pl.loop(0, CHUNKS)
+        def _(c):
+            c_copy(2, c).wait_recv()
+            c_copy(2, c, True).start()
+
+        w_tell(1).wait_recv()
+        accept(1)
+        join()
+
+    def p_copy(i, j):
+        return pltpu.make_async_remote_copy(
+            src_ref=part.at[i, j - 1], dst_ref=come.at[i, j - 1],
+            send_sem=p_s.at[i, j - 1], recv_sem=p_r.at[i, j - 1],
+            device_id=b_peer(j), device_id_type=MESH,
+        )
+
     def project(i):
         for j in (1, 3):
             f_copy(i, j).wait_recv()
@@ -265,9 +313,9 @@
             p_copy(i, j).start()
         own[i] = dot(heads, wg[b])
 
-    @pl.loop(0, AHEAD)
-    def _(i):
-        gate(i)
+    @pl.when(z > 0)
+    def _():
+        start_gates()
 
     @pl.loop(0, TILES + 1)
     def _(i):
@@ -283,9 +331,21 @@
         def _():
             for c in own_w:
                 c.wait()
-            for c in range(SIDE):
-                for j in (1, 2, 3):
-                    w_copy(j, c).wait_recv()
+
+            @pl.when(z < 4)
+            def _():
+                for j, c in order:
+                    for u in (0, 1):
+                        x_copy(u, j, c, True).wait_recv()
+
+            @pl.when((z == 5) | (z == 6))
+            def _():
+                share(())
+
+            @pl.when(z >= 4)
+            def _():
+                for j, c in order:
+                    w_copy(j, c, True).wait_recv()
 
         @pl.when(i > 0)
         def _():
@@ -300,9 +360,25 @@
             total = total + come[i, j - 1].astype(F32)
         o_ref[pl.ds(pl.multiple_of(i * TILE, TILE), TILE), :] = total.astype(BF16)
 
-    for c in range(SIDE):
-        for j in (1, 2, 3):
-            w_copy(j, c).wait_send()
+    def shared(u):
+        for j, c in order:
+            x_copy(u, j, c).wait_send()
+
+    for j, c in order:
+        w_copy(j, c).wait_send()
+
+    @pl.when(z >= 4)
+    def _():
+        for j, c in order:
+            w_copy(j, c, True).wait_send()
+
+    @pl.when((z <= 2) | (z == 7))
+    def _():
+        shared(0)
+
+    @pl.when((z >= 1) & (z <= 4))
+    def _():
+        shared(1)
 
     def sent(s):
         for c in range(CHUNKS):
@@ -336,12 +412,12 @@
 
 def layer(queries, keys, values, gates, decay_log, out_weight):
     dma = pltpu.SemaphoreType.DMA
-    anywhere = pl.BlockSpec(memory_space=pl.ANY)
+    hbm = pl.BlockSpec(memory_space=pltpu.HBM)
     vmem = pl.BlockSpec(memory_space=pltpu.VMEM)
     return pl.pallas_call(
         kernel,
         out_shape=jax.ShapeDtypeStruct((BLOCK, COLS), BF16),
-        in_specs=[anywhere] * 4 + [vmem, anywhere],
+        in_specs=[hbm] * 4 + [vmem, hbm],
         out_specs=vmem,
         scratch_shapes=[
             pltpu.VMEM((BLOCK, DK), BF16),
@@ -362,7 +438,8 @@
             pltpu.VMEM((TILES, 3, TILE, COLS), BF16),
             pltpu.VMEM((TILES, TILE, COLS), F32),
             dma((8,)),
-            dma((3, SIDE)), dma((3, SIDE)),
+            dma((2, 3, 2)), dma((2, 3, 2)),
+            dma((2, 3, 2)), dma((2, 3, 2)),
             dma((3, CHUNKS)), dma((3, CHUNKS)),
             dma((3,)), dma((3,)),
             dma((TILES, 2)), dma((TILES, 2)),
@@ -370,7 +447,7 @@
             dma((TILES, 3)), dma((TILES, 3)),
         ],
         compiler_params=pltpu.CompilerParams(
-            collective_id=0, has_side_effects=True, vmem_limit_bytes=60 * 2**20
+            collective_id=0, has_side_effects=True, vmem_limit_bytes=53 * 2**20
         ),
         cost_estimate=pl.CostEstimate(
             flops=7 * 10**9, bytes_accessed=8 * 2**20, transcendentals=2 * 2**20

time: 73.6 us -> 68 us (0.924)
  the two profiles are of different devices: /device:TPU:6 before, /device:TPU:224 now
where the time goes in v4:
time: 68 us; the launch traced here: 66.8 us
  Pallas kernels  65.3 us (96%)
  local copies, waits for them, and re-layouts  1.48 us (2%)
    pallas_call x1, Pallas kernels, layer(): pl.pallas_call(kernel, out_shape=jax.ShapeDtypeStruct((BLOCK, COLS), BF16...  65.3 us
    unnamed x3, local copies, waits for them, and re-layouts  1.48 us

profile of v4, /device:TPU:224, one launch (start us, length us, event | category | flops | bytes accessed | tf_op | source)
XLA Modules:
  0.0 66.8 jit_solution(8891863091728122901)
XLA Ops:
  0.0 0.0 copy-start
  0.0 0.7 %copy-done = f32[1,1024]{1,0:T(1,128)S(1)} copy-done((f32[1,1024]{1,0:T(1,128)S(1)}, f32[1,1024]{1,0:T(1,128)}, u32[]{:S(2)}) %copy-start) | copy-done | bytes 4120
  0.7 65.3 %retention.1 = bf16[1024,256]{1,0:T(8,128)(2,1)S(1)} custom-call(bf16[1024,256]{1,0:T(8,128)(2,1)} %q_hbm.1, bf16[1024,256]{1,0:T(8,128)(2,1)} %k_hbm.1, bf16[1024,512]{1,0:T(8,128)(2,1)} %v_hbm.1, bf16[1024,512]{1,0:T(8,128)(2,1)} %g_hbm.1, f32[1,1024]{1,0:T(1,128)S(1)} %copy-done, bf16[512,4096]{1,0:T(8,128)(2,1)} %w_hbm.1), custom_call_target="tpu_custom_call" | custom-call | flops 7000000000 | bytes 8388608 | tf_op jit(solution)/shard_map/retention/pallas_call | solution.py:417
  66.0 0.8 %copy.8 = bf16[1024,256]{1,0:T(8,128)(2,1)} copy(bf16[1024,256]{1,0:T(8,128)(2,1)S(1)} %retention.1) | data formatting | bytes 1048576
Async XLA Ops:
  0.0 0.7 %copy-start = (f32[1,1024]{1,0:T(1,128)S(1)}, f32[1,1024]{1,0:T(1,128)}, u32[]{:S(2)}) copy-start(f32[1,1024]{1,0:T(1,128)} %d_ref.1) | copy-start | bytes 12292

commit v5 on v4

--- a/solution.py
+++ b/solution.py
@@ -13,7 +13,10 @@
 COLS = 256
 TILE = 256
 TILES = BLOCK // TILE
-AHEAD = 2
+SPAN = 256
+SPANS = BLOCK // SPAN
+AHEAD = 3
+LAG = 3
 CHUNKS = 16
 ROWS = DK // CHUNKS
 
@@ -56,7 +59,7 @@
         pltpu.make_async_copy(src, dst, ld.at[i])
         for i, (src, dst) in enumerate(((k_hbm, k), (v_hbm, v), (q_hbm, q), (g_hbm, g)))
     ]
-    for c in loads:
+    for c in loads[:2]:
         c.start()
     a_rows = pl.ds(pl.multiple_of(a * DV, DV), DV)
 
@@ -67,8 +70,6 @@
         pltpu.make_async_copy(w_hbm.at[:, w_cols(a, c)], wg.at[c, a_rows], ld.at[4 + c])
         for c in range(SIDE)
     ]
-    for c in own_w:
-        c.start()
     parity = z % 2
     order = [(j, c) for c in (0, 1) for j in (2, 1, 3)]
 
@@ -111,6 +112,7 @@
 
     loads[0].wait()
     loads[1].wait()
+    loads[2].start()
     weighted = (k[...].astype(F32) * jnp.exp(last - col[...])).astype(BF16)
     state[...] = dot(weighted, v[...], ((0,), (0,)))
 
@@ -190,19 +192,22 @@
         for j, c in order:
             w_copy(j, c, True).start()
 
+    loads[3].start()
+    for c in own_w:
+        c.start()
     loads[2].wait()
-    t_at = lax.broadcasted_iota(jnp.int32, (TILE, TILE), 0)
-    s_at = lax.broadcasted_iota(jnp.int32, (TILE, TILE), 1)
-    for i in range(TILES):
-        mine = slice(i * TILE, (i + 1) * TILE)
+    t_at = lax.broadcasted_iota(jnp.int32, (SPAN, SPAN), 0)
+    s_at = lax.broadcasted_iota(jnp.int32, (SPAN, SPAN), 1)
+    for i in range(SPANS):
+        mine = slice(i * SPAN, (i + 1) * SPAN)
         for j in range(i + 1):
-            theirs = slice(j * TILE, (j + 1) * TILE)
+            theirs = slice(j * SPAN, (j + 1) * SPAN)
             spread = col[mine, :] - cum_row[:, theirs]
             if i == j:
                 spread = jnp.where(t_at >= s_at, spread, -1e30)
             scores = dot(q[mine, :], k[theirs, :], ((1,), (1,)))
             prob[:, theirs] = (scores * jnp.exp(spread)).astype(BF16)
-        upto = (i + 1) * TILE
+        upto = (i + 1) * SPAN
         ret[mine, :] = dot(prob[:, :upto], v[:upto, :])
 
     loads[3].wait()
@@ -317,7 +322,7 @@
     def _():
         start_gates()
 
-    @pl.loop(0, TILES + 1)
+    @pl.loop(0, TILES + LAG)
     def _(i):
         @pl.when(i < TILES)
         def _():
@@ -327,7 +332,7 @@
         def _():
             gate(i + AHEAD)
 
-        @pl.when(i == 1)
+        @pl.when(i == LAG)
         def _():
             for c in own_w:
                 c.wait()
@@ -347,9 +352,9 @@
                 for j, c in order:
                     w_copy(j, c, True).wait_recv()
 
-        @pl.when(i > 0)
+        @pl.when(i >= LAG)
         def _():
-            project(i - 1)
+            project(i - LAG)
 
     @pl.loop(0, TILES)
     def _(i):
@@ -431,7 +436,7 @@
             pltpu.VMEM((3, DK, DV), BF16),
             pltpu.VMEM((3, 8, 128), F32),
             pltpu.VMEM((3, 8, 128), F32),
-            pltpu.VMEM((TILE, BLOCK), BF16),
+            pltpu.VMEM((SPAN, BLOCK), BF16),
             pltpu.VMEM((BLOCK, DV), F32),
             pltpu.VMEM((TILES, TILE, SIDE * DV), BF16),
             pltpu.VMEM((TILES, 3, TILE, COLS), BF16),

time: 68 us -> 62.8 us (0.924); the launches traced: 66.8 us -> 62.4 us
  Pallas kernels: 65.3 us -> 60.9 us
    pallas_call x1, Pallas kernels: 65.3 us -> 60.9 us  [layer(): pl.pallas_call(kernel, out_shape=jax.ShapeDtypeStruct((BLOCK, COLS), BF16...]
where the time goes in v5:
time: 62.8 us; the launch traced here: 62.4 us
  Pallas kernels  60.9 us (97%)
  local copies, waits for them, and re-layouts  1.48 us (2%)
    pallas_call x1, Pallas kernels, layer(): pl.pallas_call(kernel, out_shape=jax.ShapeDtypeStruct((BLOCK, COLS), BF16...  60.9 us
    unnamed x3, local copies, waits for them, and re-layouts  1.48 us

profile of v5, /device:TPU:224, one launch (start us, length us, event | category | flops | bytes accessed | tf_op | source)
XLA Modules:
  0.0 62.4 jit_solution(16083322467970835718)
XLA Ops:
  0.0 0.0 copy-start
  0.0 0.7 %copy-done = f32[1,1024]{1,0:T(1,128)S(1)} copy-done((f32[1,1024]{1,0:T(1,128)S(1)}, f32[1,1024]{1,0:T(1,128)}, u32[]{:S(2)}) %copy-start) | copy-done | bytes 4120
  0.7 60.9 %retention.1 = bf16[1024,256]{1,0:T(8,128)(2,1)S(1)} custom-call(bf16[1024,256]{1,0:T(8,128)(2,1)} %q_hbm.1, bf16[1024,256]{1,0:T(8,128)(2,1)} %k_hbm.1, bf16[1024,512]{1,0:T(8,128)(2,1)} %v_hbm.1, bf16[1024,512]{1,0:T(8,128)(2,1)} %g_hbm.1, f32[1,1024]{1,0:T(1,128)S(1)} %copy-done, bf16[512,4096]{1,0:T(8,128)(2,1)} %w_hbm.1), custom_call_target="tpu_custom_call" | custom-call | flops 7000000000 | bytes 8388608 | tf_op jit(solution)/shard_map/retention/pallas_call | solution.py:422
  61.6 0.8 %copy.8 = bf16[1024,256]{1,0:T(8,128)(2,1)} copy(bf16[1024,256]{1,0:T(8,128)(2,1)S(1)} %retention.1) | data formatting | bytes 1048576
Async XLA Ops:
  0.0 0.7 %copy-start = (f32[1,1024]{1,0:T(1,128)S(1)}, f32[1,1024]{1,0:T(1,128)}, u32[]{:S(2)}) copy-start(f32[1,1024]{1,0:T(1,128)} %d_ref.1) | copy-start | bytes 12292

commit v6 on v5

--- a/solution.py
+++ b/solution.py
@@ -96,6 +96,13 @@
             for u in halves:
                 x_copy(u, j, c).start()
 
+    @pl.when(z >= 4)
+    def _():
+        pl.semaphore_wait(barrier, 8)
+        for other in (False, True):
+            for j, c in order:
+                w_copy(j, c, other).start()
+
     lane = lax.broadcasted_iota(jnp.int32, (8, 128), 1)
     run = jnp.concatenate([d_ref[:, 128 * r : 128 * (r + 1)] for r in range(8)], axis=0)
     for s in (1, 2, 4, 8, 16, 32, 64):
@@ -169,7 +176,9 @@
     def join():
         into[0] = (into[1].astype(F32) + told[1, 0:1, 0:1] * into[2].astype(F32)).astype(BF16)
 
-    pl.semaphore_wait(barrier, 8)
+    @pl.when(z < 4)
+    def _():
+        pl.semaphore_wait(barrier, 8)
 
     @pl.when(z == 0)
     def _():
@@ -184,13 +193,10 @@
     def _():
         source(2)
 
-    for j, c in order:
-        w_copy(j, c).start()
-
-    @pl.when(z >= 4)
+    @pl.when(z < 4)
     def _():
         for j, c in order:
-            w_copy(j, c, True).start()
+            w_copy(j, c).start()
 
     loads[3].start()
     for c in own_w:

time: 62.8 us -> 62 us (0.987)
  Pallas kernels: 60.9 us -> 59.9 us
    pallas_call x1, Pallas kernels: 60.9 us -> 59.9 us  [layer(): pl.pallas_call(kernel, out_shape=jax.ShapeDtypeStruct((BLOCK, COLS), BF16...]
where the time goes in v6:
time: 62 us; the launch traced here: 61.3 us
  Pallas kernels  59.9 us (97%)
  local copies, waits for them, and re-layouts  1.48 us (2%)
    pallas_call x1, Pallas kernels, layer(): pl.pallas_call(kernel, out_shape=jax.ShapeDtypeStruct((BLOCK, COLS), BF16...  59.9 us
    unnamed x3, local copies, waits for them, and re-layouts  1.48 us

profile of v6, /device:TPU:224, one launch (start us, length us, event | category | flops | bytes accessed | tf_op | source)
XLA Modules:
  0.0 61.3 jit_solution(17085695141565462889)
XLA Ops:
  0.0 0.0 copy-start
  0.0 0.7 %copy-done = f32[1,1024]{1,0:T(1,128)S(1)} copy-done((f32[1,1024]{1,0:T(1,128)S(1)}, f32[1,1024]{1,0:T(1,128)}, u32[]{:S(2)}) %copy-start) | copy-done | bytes 4120
  0.7 59.9 %retention.1 = bf16[1024,256]{1,0:T(8,128)(2,1)S(1)} custom-call(bf16[1024,256]{1,0:T(8,128)(2,1)} %q_hbm.1, bf16[1024,256]{1,0:T(8,128)(2,1)} %k_hbm.1, bf16[1024,512]{1,0:T(8,128)(2,1)} %v_hbm.1, bf16[1024,512]{1,0:T(8,128)(2,1)} %g_hbm.1, f32[1,1024]{1,0:T(1,128)S(1)} %copy-done, bf16[512,4096]{1,0:T(8,128)(2,1)} %w_hbm.1), custom_call_target="tpu_custom_call" | custom-call | flops 7000000000 | bytes 8388608 | tf_op jit(solution)/shard_map/retention/pallas_call | solution.py:428
  60.6 0.8 %copy.8 = bf16[1024,256]{1,0:T(8,128)(2,1)} copy(bf16[1024,256]{1,0:T(8,128)(2,1)S(1)} %retention.1) | data formatting | bytes 1048576
Async XLA Ops:
  0.0 0.7 %copy-start = (f32[1,1024]{1,0:T(1,128)S(1)}, f32[1,1024]{1,0:T(1,128)}, u32[]{:S(2)}) copy-start(f32[1,1024]{1,0:T(1,128)} %d_ref.1) | copy-start | bytes 12292

commit v7 on v6

--- a/solution.py
+++ b/solution.py
@@ -17,7 +17,7 @@
 SPANS = BLOCK // SPAN
 AHEAD = 3
 LAG = 3
-CHUNKS = 16
+CHUNKS = 8
 ROWS = DK // CHUNKS
 
 

time: 62 us -> 61.8 us (level)
  no operation moved by 1% of the time
where the time goes in v7:
time: 61.8 us; the launch traced here: 60.9 us
  Pallas kernels  59.4 us (96%)
  local copies, waits for them, and re-layouts  1.48 us (2%)
    pallas_call x1, Pallas kernels, layer(): pl.pallas_call(kernel, out_shape=jax.ShapeDtypeStruct((BLOCK, COLS), BF16...  59.4 us
    unnamed x3, local copies, waits for them, and re-layouts  1.48 us

profile of v7, /device:TPU:224, one launch (start us, length us, event | category | flops | bytes accessed | tf_op | source)
XLA Modules:
  0.0 60.9 jit_solution(6908028873466141650)
XLA Ops:
  0.0 0.0 copy-start
  0.0 0.7 %copy-done = f32[1,1024]{1,0:T(1,128)S(1)} copy-done((f32[1,1024]{1,0:T(1,128)S(1)}, f32[1,1024]{1,0:T(1,128)}, u32[]{:S(2)}) %copy-start) | copy-done | bytes 4120
  0.7 59.4 %retention.1 = bf16[1024,256]{1,0:T(8,128)(2,1)S(1)} custom-call(bf16[1024,256]{1,0:T(8,128)(2,1)} %q_hbm.1, bf16[1024,256]{1,0:T(8,128)(2,1)} %k_hbm.1, bf16[1024,512]{1,0:T(8,128)(2,1)} %v_hbm.1, bf16[1024,512]{1,0:T(8,128)(2,1)} %g_hbm.1, f32[1,1024]{1,0:T(1,128)S(1)} %copy-done, bf16[512,4096]{1,0:T(8,128)(2,1)} %w_hbm.1), custom_call_target="tpu_custom_call" | custom-call | flops 7000000000 | bytes 8388608 | tf_op jit(solution)/shard_map/retention/pallas_call | solution.py:428
  60.1 0.8 %copy.8 = bf16[1024,256]{1,0:T(8,128)(2,1)} copy(bf16[1024,256]{1,0:T(8,128)(2,1)S(1)} %retention.1) | data formatting | bytes 1048576
Async XLA Ops:
  0.0 0.7 %copy-start = (f32[1,1024]{1,0:T(1,128)S(1)}, f32[1,1024]{1,0:T(1,128)}, u32[]{:S(2)}) copy-start(f32[1,1024]{1,0:T(1,128)} %d_ref.1) | copy-start | bytes 12292

commit v8 on v7

--- a/solution.py
+++ b/solution.py
@@ -15,8 +15,8 @@
 TILES = BLOCK // TILE
 SPAN = 256
 SPANS = BLOCK // SPAN
-AHEAD = 3
-LAG = 3
+AHEAD = 4
+LAG = 4
 CHUNKS = 8
 ROWS = DK // CHUNKS
 

time: 61.8 us -> 61.8 us (level)
  no operation moved by 1% of the time
where the time goes in v8:
time: 61.8 us; the launch traced here: 60.9 us
  Pallas kernels  59.4 us (96%)
  local copies, waits for them, and re-layouts  1.48 us (2%)
    pallas_call x1, Pallas kernels, layer(): pl.pallas_call(kernel, out_shape=jax.ShapeDtypeStruct((BLOCK, COLS), BF16...  59.4 us
    unnamed x3, local copies, waits for them, and re-layouts  1.48 us

profile of v8, /device:TPU:224, one launch (start us, length us, event | category | flops | bytes accessed | tf_op | source)
XLA Modules:
  0.0 60.9 jit_solution(4314850669136088594)
XLA Ops:
  0.0 0.0 copy-start
  0.0 0.7 %copy-done = f32[1,1024]{1,0:T(1,128)S(1)} copy-done((f32[1,1024]{1,0:T(1,128)S(1)}, f32[1,1024]{1,0:T(1,128)}, u32[]{:S(2)}) %copy-start) | copy-done | bytes 4120
  0.7 59.4 %retention.1 = bf16[1024,256]{1,0:T(8,128)(2,1)S(1)} custom-call(bf16[1024,256]{1,0:T(8,128)(2,1)} %q_hbm.1, bf16[1024,256]{1,0:T(8,128)(2,1)} %k_hbm.1, bf16[1024,512]{1,0:T(8,128)(2,1)} %v_hbm.1, bf16[1024,512]{1,0:T(8,128)(2,1)} %g_hbm.1, f32[1,1024]{1,0:T(1,128)S(1)} %copy-done, bf16[512,4096]{1,0:T(8,128)(2,1)} %w_hbm.1), custom_call_target="tpu_custom_call" | custom-call | flops 7000000000 | bytes 8388608 | tf_op jit(solution)/shard_map/retention/pallas_call | solution.py:428
  60.1 0.8 %copy.8 = bf16[1024,256]{1,0:T(8,128)(2,1)} copy(bf16[1024,256]{1,0:T(8,128)(2,1)S(1)} %retention.1) | data formatting | bytes 1048576
Async XLA Ops:
  0.0 0.7 %copy-start = (f32[1,1024]{1,0:T(1,128)S(1)}, f32[1,1024]{1,0:T(1,128)}, u32[]{:S(2)}) copy-start(f32[1,1024]{1,0:T(1,128)} %d_ref.1) | copy-start | bytes 12292
